TPU v7x, 32 devices: a whole 2x2x4 slice. The times are simulated.
32 devices in a mesh: dp: 2 (over core), section: 2 (over x), mp: 8 (over z, y).
Axes of the slice: x: 2, y: 2, z: 4, core: 2. Of those that a mesh axis runs over, the one named last changes fastest.
Arguments:
- activations: bfloat16 [2, 2, 128, 32, 384], P('dp', 'section', 'mp'), may hold values from -8 to 8
- out_grads: bfloat16 [2, 2, 128, 32, 384], P('dp', 'section', 'mp'), may hold values from -6 to 6
- layer_weights: bfloat16 [2, 4, 384, 384], P('section'), may hold values from -1.5 to 1.5
Outputs:
- received: bfloat16 [2, 2, 128, 32, 384], P('dp', 'section', 'mp')
- weight_grads: float32 [2, 4, 384, 384], P('section', 'dp', 'mp')
All inputs are finite; a program needn't handle non-finite values.
Results may differ from a plain program's by a relative error of at most 0.011.
Values may be sent and summed in bfloat16 or wider, within the bound.
A program may use at most 64 MiB of HBM per device.

v0:
```python
import jax
import jax.numpy as jnp
from jax import lax
from jax.sharding import PartitionSpec as P

HEAD_DIM = 64


EPS = 1e-05


def passed_along(array, axis, by):
    peers = lax.axis_size(axis)
    pairs = [(i, i + by) for i in range(peers) if 0 <= i + by < peers]
    return lax.ppermute(array, axis, pairs)


def normalize(values):
    mean_value = jnp.mean(values, axis=-1, keepdims=True)
    centred = values - mean_value
    inverse = lax.rsqrt(jnp.mean(centred * centred, axis=-1, keepdims=True) + EPS)
    return (centred * inverse, inverse)


def norm_backward(grad_in, standard, inverse):
    grad_mean = jnp.mean(grad_in, axis=-1, keepdims=True)
    grad_proj = jnp.mean(grad_in * standard, axis=-1, keepdims=True)
    return inverse * (grad_in - grad_mean - standard * grad_proj)


def attend(queries, key_rows, values_in, out_delta):
    seq_count, res_count, head_width = queries.shape
    head_shape = (seq_count, res_count, head_width // HEAD_DIM, HEAD_DIM)
    query_heads = queries.reshape(head_shape)
    key_heads = key_rows.reshape(head_shape)
    value_heads = values_in.reshape(head_shape)
    delta_heads = out_delta.reshape(head_shape)
    scaling = HEAD_DIM ** (-0.5)
    scores = (
        jnp.einsum("srhe,trhe->rhst", query_heads, key_heads, preferred_element_type=jnp.float32)
        * scaling
    )
    row_max = jnp.max(scores, axis=-1, keepdims=True)
    exponent = jnp.exp(scores - row_max)
    probs = exponent / jnp.sum(exponent, axis=-1, keepdims=True)
    soft = probs.astype(jnp.bfloat16)
    attn_out = jnp.einsum(
        "rhst,trhe->srhe", soft, value_heads, preferred_element_type=jnp.float32
    ).astype(jnp.bfloat16)
    dprobs = jnp.einsum(
        "srhe,trhe->rhst", delta_heads, value_heads, preferred_element_type=jnp.float32
    )
    row_delta = jnp.sum(probs * dprobs, axis=-1, keepdims=True)
    dscores = (probs * (dprobs - row_delta)).astype(jnp.bfloat16)
    query_grad = (
        jnp.einsum("rhst,trhe->srhe", dscores, key_heads, preferred_element_type=jnp.float32)
        * scaling
    ).astype(jnp.bfloat16)
    key_grad = (
        jnp.einsum("rhst,srhe->trhe", dscores, query_heads, preferred_element_type=jnp.float32)
        * scaling
    ).astype(jnp.bfloat16)
    value_grad = jnp.einsum(
        "rhst,srhe->trhe", soft, delta_heads, preferred_element_type=jnp.float32
    ).astype(jnp.bfloat16)
    flat_shape = (seq_count, res_count, head_width)
    return (
        attn_out.reshape(flat_shape),
        jnp.stack(
            [
                query_grad.reshape(flat_shape),
                key_grad.reshape(flat_shape),
                value_grad.reshape(flat_shape),
            ]
        ),
    )


def input_gradient(dprojected, weight, standard, inverse, out_flat):
    normed_grad = jnp.einsum(
        "nth,ndh->td", dprojected, weight[:3], preferred_element_type=jnp.float32
    )
    branch = lax.optimization_barrier(
        norm_backward(normed_grad, standard, inverse).astype(jnp.bfloat16)
    )
    return (out_flat.astype(jnp.float32) + branch.astype(jnp.float32)).astype(jnp.bfloat16)


def per_device(activations, out_grads, layer_weights):
    weight = layer_weights[0]
    model_width = activations.shape[4]
    head_width = weight.shape[2]
    col_acts, col_grads = (
        lax.all_to_all(activations, "mp", split_axis=3, concat_axis=2, tiled=True),
        lax.all_to_all(out_grads, "mp", split_axis=3, concat_axis=2, tiled=True),
    )
    seq_count, res_count = (col_acts.shape[2], col_acts.shape[3])
    tokens = seq_count * res_count
    standard, inverse = normalize(col_acts.reshape(tokens, model_width).astype(jnp.float32))
    normed = standard.astype(jnp.bfloat16)
    out_flat = col_grads.reshape(tokens, model_width)
    projected = jnp.einsum(
        "td,ndh->nth", normed, weight[:3], preferred_element_type=jnp.float32
    ).astype(jnp.bfloat16)
    attn_grad = jnp.dot(out_flat, weight[3], preferred_element_type=jnp.float32).astype(
        jnp.bfloat16
    )
    grid_shape = (seq_count, res_count, head_width)
    attn_out, stacked_grads = attend(
        projected[0].reshape(grid_shape),
        projected[1].reshape(grid_shape),
        projected[2].reshape(grid_shape),
        attn_grad.reshape(grid_shape),
    )
    dprojected = stacked_grads.reshape(3, tokens, head_width)
    attn_flat = attn_out.reshape(tokens, head_width)
    input_grad = input_gradient(dprojected, weight, standard, inverse, out_flat)
    row_grads = lax.all_to_all(
        input_grad.reshape(col_acts.shape), "mp", split_axis=2, concat_axis=3, tiled=True
    )
    received = passed_along(row_grads, "section", -1)
    projection_terms = jnp.einsum(
        "td,nth->ndh", normed, dprojected, preferred_element_type=jnp.float32
    )
    output_term = jnp.einsum("td,th->dh", out_flat, attn_flat, preferred_element_type=jnp.float32)
    grad_term = jnp.concatenate([projection_terms, output_term[None]], axis=0)[None]
    model_part = lax.psum_scatter(grad_term, "mp", scatter_dimension=2, tiled=True)
    replica_part = lax.psum_scatter(model_part, "dp", scatter_dimension=1, tiled=True)
    return (received, replica_part)


def solution(mesh):
    in_specs = (
        P("dp", "section", "mp", None, None),
        P("dp", "section", "mp", None, None),
        P("section", None, None, None),
    )
    out_specs = (P("dp", "section", "mp", None, None), P("section", "dp", "mp", None))
    return jax.shard_map(
        per_device, mesh=mesh, in_specs=in_specs, out_specs=out_specs, check_vma=False
    )
```

profile of v0, /device:TPU:0, one launch (start us, length us, event | category | flops | bytes accessed | tf_op | source)
XLA Modules:
  0.0 215.8 jit_solution(4491237370421747592)
XLA Ops:
  7.2 1.9 copy.81
  9.1 7.3 %all-to-all-start.1 = ((bf16[1,1,16,32,384]{4,2,1,0,3:T(8,128)(2,1)}), bf16[1,1,16,32,384]{4,2,1,0,3:T(8,128)(2,1)S(1)}, u32[]{:S(2)}, u32[]{:S(2)}) async-start(bf16[1,1,16,32,384]{4,2,1,0,3:T(8,128)(2,1)} %copy.81), calls=%async_computation.1 | async-start | bytes 786432 | tf_op jit(solution)/shard_map/all_to_all | solution.py:94
  16.4 0.9 copy.78
  17.3 10.8 %all-to-all-done.1 = bf16[1,1,16,32,384]{4,2,1,0,3:T(8,128)(2,1)S(1)} async-done(((bf16[1,1,16,32,384]{4,2,1,0,3:T(8,128)(2,1)}), bf16[1,1,16,32,384]{4,2,1,0,3:T(8,128)(2,1)S(1)}, u32[]{:S(2)}, u32[]{:S(2)}) %all-to-all-start.1) | async-done | bytes 393248 | tf_op jit(solution)/shard_map/all_to_all | solution.py:94
  28.1 3.6 %all-to-all-start = ((bf16[1,1,16,32,384]{4,2,1,0,3:T(8,128)(2,1)}), bf16[1,1,16,32,384]{4,2,1,0,3:T(8,128)(2,1)S(1)}, u32[]{:S(2)}, u32[]{:S(2)}) async-start(bf16[1,1,16,32,384]{4,2,1,0,3:T(8,128)(2,1)} %copy.78), calls=%async_computation | async-start | bytes 786432 | tf_op jit(solution)/shard_map/all_to_all | solution.py:95
  31.8 0.2 copy.123
  32.0 0.4 fusion.25
  32.4 0.6 multiply_reduce_fusion.2
  32.9 0.1 div.27
  33.1 0.1 rsqrt.13
  33.2 0.4 multiply_convert_fusion.2
  33.6 0.1 reshape.94
  33.7 2.0 fusion.3
  35.7 0.1 fusion.27
  35.8 0.6 reshape_reshape_squeeze.9
  36.4 1.6 copy.87
  38.0 0.6 reshape_reshape_squeeze.10
  38.6 0.9 copy.83
  39.5 3.8 %all-to-all-done = bf16[1,1,16,32,384]{4,2,1,0,3:T(8,128)(2,1)S(1)} async-done(((bf16[1,1,16,32,384]{4,2,1,0,3:T(8,128)(2,1)}), bf16[1,1,16,32,384]{4,2,1,0,3:T(8,128)(2,1)S(1)}, u32[]{:S(2)}, u32[]{:S(2)}) %all-to-all-start) | async-done | bytes 393248 | tf_op jit(solution)/shard_map/all_to_all | solution.py:95
  43.3 0.2 copy.124
  43.5 1.4 convolution_convert_fusion.3
  44.9 0.6 reshape_reshape.6
  45.5 1.6 copy.85
  47.1 0.6 reshape_reshape_squeeze.11
  47.7 1.6 copy.86
  49.3 1.3 fusion.28
  50.6 1.6 multiply_reduce_fusion
  52.2 0.4 multiply_convert_fusion
  52.6 1.1 fusion.7
  53.7 1.4 fusion.6
  55.1 1.4 fusion.8
  56.5 1.1 fusion.9
  57.6 0.3 reshape.91
  57.8 0.4 copy.96
  58.3 0.3 copy-done.5
  58.6 1.6 copy.89
  60.2 0.6 stack.9
  60.8 2.4 %copy.92 = bf16[128,4,6,64]{3,2,1,0:T(8,128)(2,1)S(1)} copy(bf16[128,4,6,64]{0,3,2,1:T(8,128)(2,1)} %fusion.6) | data formatting | bytes 786432 | tf_op jit(solution)/shard_map/convert_element_type | solution.py:62
  63.3 1.4 stack.10
  64.6 2.4 %copy.95 = bf16[128,4,6,64]{3,2,1,0:T(8,128)(2,1)S(1)} copy(bf16[128,4,6,64]{0,3,2,1:T(8,128)(2,1)} %fusion.8) | data formatting | bytes 786432 | tf_op jit(solution)/shard_map/convert_element_type | solution.py:65
  67.0 1.4 stack.11
  68.4 2.4 %copy.104 = bf16[128,4,6,64]{3,2,1,0:T(8,128)(2,1)S(1)} copy(bf16[128,4,6,64]{0,3,2,1:T(8,128)(2,1)} %fusion.9) | data formatting | bytes 786432 | tf_op jit(solution)/shard_map/convert_element_type | solution.py:49
  70.8 1.4 reshape_reshape.7
  72.2 1.5 convolution_bitcast_fusion.2
  73.8 1.0 copy-done
  74.9 0.8 convolution_bitcast_fusion
  75.7 0.2 maximum_bitcast_fusion
  75.8 2.5 %copy.105 = f32[1,4,384,384]{3,1,0,2:T(4,128)} copy(f32[1,4,384,384]{2,3,1,0:T(8,128)S(1)} %maximum_bitcast_fusion) | data formatting | bytes 4718592 | tf_op jit(solution)/shard_map/broadcast_in_dim | solution.py:126
  78.3 0.2 copy.80
  78.5 1.0 copy-done.1
  79.6 1.9 fusion.26
  81.5 0.2 multiply_convert_fusion.1
  81.7 0.1 add_convert_fusion
  81.8 0.2 copy.97
  82.0 0.8 reshape.90
  82.9 3.6 %all-to-all-start.2 = ((bf16[1,1,128,4,384]{4,3,1,0,2:T(4,128)(2,1)}), bf16[1,1,128,4,384]{4,3,1,0,2:T(4,128)(2,1)S(1)}, u32[]{:S(2)}, u32[]{:S(2)}) async-start(bf16[1,1,128,4,384]{4,3,1,0,2:T(4,128)(2,1)} %bitcast.11), calls=%async_computation.2 | async-start | bytes 786432 | tf_op jit(solution)/shard_map/all_to_all | solution.py:118
  86.6 0.6 dynamic-slice
  87.8 106.8 %all-reduce.3.cloned.1.call-done = f32[1,4,384,384]{3,1,0,2:T(4,128)} async-done(((f32[1,4,384,384]{3,1,0,2:T(4,128)}), f32[1,4,384,384]{3,1,0,2:T(4,128)}) %all-reduce.3.cloned.1.call-update) | async-done | bytes 2359312
  194.6 1.0 constant_dynamic-slice_fusion
  195.6 0.7 copy.106
  196.4 0.1 copy.99
  196.6 1.3 collective-permute-start
  197.9 10.3 %collective-permute-done = bf16[1,1,16,32,384]{4,3,2,1,0:T(8,128)(2,1)S(1)} collective-permute-done((bf16[1,1,16,32,384]{4,3,2,1,0:T(8,128)(2,1)S(1)}, bf16[1,1,16,32,384]{4,3,2,1,0:T(8,128)(2,1)S(1)}, u32[]{:S(2)}, u32[]{:S(2)}) %collective-permute-start) | collective-permute-done | bytes 393248 | tf_op jit(solution)/shard_map/ppermute | solution.py:15
  208.3 0.7 copy.129
  (34 shorter events, 0.6 us)
Async XLA Ops:
  7.2 9.2 %copy-start.6 = (bf16[1,1,16,32,384]{4,3,2,1,0:T(8,128)(2,1)S(1)}, bf16[1,1,16,32,384]{4,3,2,1,0:T(8,128)(2,1)}, u32[]{:S(2)}) copy-start(bf16[1,1,16,32,384]{4,3,2,1,0:T(8,128)(2,1)} %param.4) | copy-start | bytes 1179652
  9.1 19.0 %all-to-all-start.1 = ((bf16[1,1,16,32,384]{4,2,1,0,3:T(8,128)(2,1)}), bf16[1,1,16,32,384]{4,2,1,0,3:T(8,128)(2,1)S(1)}, u32[]{:S(2)}, u32[]{:S(2)}) async-start(bf16[1,1,16,32,384]{4,2,1,0,3:T(8,128)(2,1)} %copy.81), calls=%async_computation.1 | async-start | bytes 786432 | tf_op jit(solution)/shard_map/all_to_all | solution.py:94
  28.1 15.2 %all-to-all-start = ((bf16[1,1,16,32,384]{4,2,1,0,3:T(8,128)(2,1)}), bf16[1,1,16,32,384]{4,2,1,0,3:T(8,128)(2,1)S(1)}, u32[]{:S(2)}, u32[]{:S(2)}) async-start(bf16[1,1,16,32,384]{4,2,1,0,3:T(8,128)(2,1)} %copy.78), calls=%async_computation | async-start | bytes 786432 | tf_op jit(solution)/shard_map/all_to_all | solution.py:95
  31.7 162.9 %all-reduce.3.cloned.1.call-start = ((), (), s32[]{:S(2)}) async-start(), calls=%async_computation.5 | async-start | bytes 4718592
  47.1 2.2 %copy-start.4 = (bf16[128,4,6,64]{0,3,2,1:T(8,128)(2,1)S(1)}, bf16[128,4,6,64]{0,3,2,1:T(8,128)(2,1)}, u32[]{:S(2)}) copy-start(bf16[128,4,6,64]{0,3,2,1:T(8,128)(2,1)} %copy.87) | copy-start | bytes 1179652
  50.6 1.6 copy-start.9
  52.5 2.5 %copy-start.7 = (bf16[128,4,6,64]{0,3,2,1:T(8,128)(2,1)S(1)}, bf16[128,4,6,64]{0,3,2,1:T(8,128)(2,1)}, u32[]{:S(2)}) copy-start(bf16[128,4,6,64]{0,3,2,1:T(8,128)(2,1)} %copy.85) | copy-start | bytes 1179652
  55.1 1.4 copy-start.8
  57.6 1.0 copy-start.5
  72.2 1.5 copy-start.2
  72.2 1.5 copy-start.3
  73.8 1.1 copy-start
  78.3 1.3 copy-start.1
  81.7 4.9 %copy-start.10 = (u32[32]{0:T(128)S(1)}, u32[32]{0:T(128)}, u32[]{:S(2)}) copy-start(u32[32]{0:T(128)} %constant.20) | copy-start | bytes 388
  82.9 113.5 %all-to-all-start.2 = ((bf16[1,1,128,4,384]{4,3,1,0,2:T(4,128)(2,1)}), bf16[1,1,128,4,384]{4,3,1,0,2:T(4,128)(2,1)S(1)}, u32[]{:S(2)}, u32[]{:S(2)}) async-start(bf16[1,1,128,4,384]{4,3,1,0,2:T(4,128)(2,1)} %bitcast.11), calls=%async_computation.2 | async-start | bytes 786432 | tf_op jit(solution)/shard_map/all_to_all | solution.py:118
  86.5 121.8 %reduce-scatter.2.cloned.1.call-start = ((), (), s32[]{:S(2)}) async-start(), calls=%async_computation.4 | async-start | bytes 442368 | tf_op jit(solution)/shard_map/reduce_scatter | solution.py:128
  196.6 11.6 %collective-permute-start = (bf16[1,1,16,32,384]{4,3,2,1,0:T(8,128)(2,1)S(1)}, bf16[1,1,16,32,384]{4,3,2,1,0:T(8,128)(2,1)S(1)}, u32[]{:S(2)}, u32[]{:S(2)}) collective-permute-start(bf16[1,1,16,32,384]{4,3,2,1,0:T(8,128)(2,1)S(1)} %all_to_all.38), channel_id=1, source_target_pairs={{8,0},{9,1},{10,2},{11,3},{12,4},{13,5},{14,6},{15,7},{24,16},{25,... | collective-permute-start | bytes 1179656 | tf_op jit(solution)/shard_map/ppermute | solution.py:15
Sparse Core Ops, SparseCore 0:
  78.4 116.1 all-reduce.2
  197.5 6.7 reduce-scatter.1
where the time goes:
time: 217 us; the launch traced here: 216 us
  waiting for transfers between devices  132 us (61%)
  local copies, waits for them, and re-layouts  35.4 us (16%)
  starting transfers between devices  15.9 us (7%)
  matrix products  15.3 us (7%)
  between operations  15.1 us (7%)
  other arithmetic  2.28 us (1%)
    unnamed x3, waiting for transfers between devices  107 us
    all_to_all x1, waiting for transfers between devices, per_device(): lax.all_to_all(activations, 'mp', split_axis=3, concat_axis=2, tiled=True)  10.8 us
    ppermute x1, waiting for transfers between devices, passed_along(): return lax.ppermute(array, axis, pairs)  10.3 us
    unnamed x29, local copies, waits for them, and re-layouts  7.64 us
    all_to_all x1, starting transfers between devices, per_device(): lax.all_to_all(activations, 'mp', split_axis=3, concat_axis=2, tiled=True)  7.28 us
  transfers between devices with their start and end apart: 6, of which 4 were waited for; matrix products, arithmetic and copies ran while one was open for 7% of the time, Pallas kernels for 0%

commit v1 on v0

--- a/solution.py
+++ b/solution.py
@@ -1,6 +1,10 @@
+import functools
+
 import jax
 import jax.numpy as jnp
 from jax import lax
+from jax.experimental import pallas as pl
+from jax.experimental.pallas import tpu as pltpu
 from jax.sharding import PartitionSpec as P
 
 HEAD_DIM = 64
@@ -86,7 +90,7 @@
     return (out_flat.astype(jnp.float32) + branch.astype(jnp.float32)).astype(jnp.bfloat16)
 
 
-def per_device(activations, out_grads, layer_weights):
+def per_device_plain(activations, out_grads, layer_weights):
     weight = layer_weights[0]
     model_width = activations.shape[4]
     head_width = weight.shape[2]
@@ -129,6 +133,315 @@
     return (received, replica_part)
 
 
+MESH = pl.DeviceIdType.MESH
+LANES = 128
+ROWS = 16
+F32 = jnp.float32
+BF16 = jnp.bfloat16
+
+
+def dot_t(left, right):
+    return lax.dot_general(left, right, (((1,), (1,)), ((), ())), preferred_element_type=F32)
+
+
+def t_dot(left, right):
+    return lax.dot_general(left, right, (((0,), (0,)), ((), ())), preferred_element_type=F32)
+
+
+def attend_pair(query, key, value, delta):
+    count = LANES // HEAD_DIM
+    seqs = query.shape[0]
+    scaling = HEAD_DIM ** (-0.5)
+    lane = lax.broadcasted_iota(jnp.int32, (seqs, LANES), 1)
+    masks = [(lane >= h * HEAD_DIM) & (lane < (h + 1) * HEAD_DIM) for h in range(count)]
+    zero = jnp.zeros_like(key)
+    keys = jnp.concatenate([jnp.where(m, key, zero) for m in masks], axis=0)
+    values = jnp.concatenate([jnp.where(m, value, zero) for m in masks], axis=0)
+    scores = dot_t(query, keys)
+    dprobs = dot_t(delta, values)
+    softs, dscores = [], []
+    for h in range(count):
+        cut = slice(h * seqs, (h + 1) * seqs)
+        score = scores[:, cut] * scaling
+        exponent = jnp.exp(score - jnp.max(score, axis=-1, keepdims=True))
+        probs = exponent * (1.0 / jnp.sum(exponent, axis=-1, keepdims=True))
+        dprob = dprobs[:, cut]
+        row_delta = jnp.sum(probs * dprob, axis=-1, keepdims=True)
+        softs.append(probs.astype(BF16))
+        dscores.append((probs * (dprob - row_delta)).astype(BF16))
+    soft = jnp.concatenate(softs, axis=1)
+    dscore = jnp.concatenate(dscores, axis=1)
+    out = jnp.dot(soft, values, preferred_element_type=F32)
+    query_grad = jnp.dot(dscore, keys, preferred_element_type=F32) * scaling
+    key_grad = t_dot(dscores[0], query)
+    value_grad = t_dot(softs[0], delta)
+    for h in range(1, count):
+        key_grad = jnp.where(masks[h], t_dot(dscores[h], query), key_grad)
+        value_grad = jnp.where(masks[h], t_dot(softs[h], delta), value_grad)
+    key_grad = key_grad * scaling
+    return query_grad.astype(BF16), key_grad.astype(BF16), value_grad.astype(BF16), out.astype(BF16)
+
+
+def kernel(
+    n_mp, n_section, n_dp, acts_ref, grads_ref, w_ref, got_ref, wout_ref,
+    cols, lefts, rights, back, part, other, mine, share, landed,
+    col_send, col_recv, back_send, back_recv, dp_send, dp_recv, mp_send, mp_recv,
+):
+    me = lax.axis_index("mp")
+    section = lax.axis_index("section")
+    replica = lax.axis_index("dp")
+    columns, _, seqs, width = acts_ref.shape
+    tokens = n_mp * seqs
+    slots = wout_ref.shape[0]
+    rows = wout_ref.shape[1]
+    sends_back = section > 0
+    gets_back = section < n_section - 1
+
+    def peer(k):
+        return lax.rem(me + k, n_mp)
+
+    def source(k):
+        return lax.rem(me + n_mp - k, n_mp)
+
+    def col_copy(which, c, k):
+        ref = acts_ref if which == 0 else grads_ref
+        return pltpu.make_async_remote_copy(
+            src_ref=ref.at[c, peer(k)], dst_ref=cols.at[which, c, me],
+            send_sem=col_send.at[which, c, k], recv_sem=col_recv.at[which, c, me],
+            device_id={"mp": peer(k)}, device_id_type=MESH)
+
+    def col_wait(which, c, k):
+        return pltpu.make_async_remote_copy(
+            src_ref=acts_ref.at[c, me], dst_ref=cols.at[which, c, source(k)],
+            send_sem=col_send.at[which, c, k], recv_sem=col_recv.at[which, c, source(k)],
+            device_id={"mp": peer(k)}, device_id_type=MESH)
+
+    def back_copy(c, p):
+        return pltpu.make_async_remote_copy(
+            src_ref=back.at[c, p], dst_ref=got_ref.at[c, me],
+            send_sem=back_send.at[c, p], recv_sem=back_recv.at[c, me],
+            device_id={"section": jnp.maximum(section - 1, 0), "mp": p}, device_id_type=MESH)
+
+    def back_wait(c, p):
+        return pltpu.make_async_remote_copy(
+            src_ref=back.at[c, p], dst_ref=got_ref.at[c, p],
+            send_sem=back_send.at[c, p], recv_sem=back_recv.at[c, p],
+            device_id={"section": jnp.maximum(section - 1, 0), "mp": p}, device_id_type=MESH)
+
+    def dp_copy(j):
+        return pltpu.make_async_remote_copy(
+            src_ref=part.at[j], dst_ref=other.at[j],
+            send_sem=dp_send.at[j], recv_sem=dp_recv.at[j],
+            device_id={"dp": 1 - replica}, device_id_type=MESH)
+
+    def mp_copy(j, k):
+        return pltpu.make_async_remote_copy(
+            src_ref=share.at[j, peer(k)], dst_ref=landed.at[j, me],
+            send_sem=mp_send.at[j, k], recv_sem=mp_recv.at[j, me],
+            device_id={"mp": peer(k)}, device_id_type=MESH)
+
+    def mp_wait(j, k):
+        return pltpu.make_async_remote_copy(
+            src_ref=share.at[j, me], dst_ref=landed.at[j, source(k)],
+            send_sem=mp_send.at[j, k], recv_sem=mp_recv.at[j, source(k)],
+            device_id={"mp": peer(k)}, device_id_type=MESH)
+
+    barrier = pltpu.get_barrier_semaphore()
+
+    @pl.loop(1, n_mp)
+    def _(k):
+        pl.semaphore_signal(barrier, inc=1, device_id={"mp": peer(k)}, device_id_type=MESH)
+
+    pl.semaphore_signal(barrier, inc=1, device_id={"dp": 1 - replica}, device_id_type=MESH)
+
+    @pl.when(sends_back)
+    def _():
+        @pl.loop(0, n_mp)
+        def _(p):
+            pl.semaphore_signal(
+                barrier, inc=1, device_id={"section": section - 1, "mp": p}, device_id_type=MESH)
+
+    @pl.when(gets_back)
+    def _():
+        @pl.loop(0, n_mp)
+        def _(p):
+            pl.semaphore_signal(
+                barrier, inc=1, device_id={"section": section + 1, "mp": p}, device_id_type=MESH)
+
+    neighbours = (section > 0).astype(jnp.int32) + (section < n_section - 1).astype(jnp.int32)
+    pl.semaphore_wait(barrier, n_mp + n_mp * neighbours)
+
+    @pl.loop(0, columns)
+    def _(c):
+        @pl.loop(1, n_mp)
+        def _(k):
+            col_copy(0, c, k).start()
+            col_copy(1, c, k).start()
+
+    @pl.loop(0, columns)
+    def _(c):
+        cols[0, c, me] = acts_ref[c, me]
+        cols[1, c, me] = grads_ref[c, me]
+
+    @pl.when(jnp.logical_not(gets_back))
+    def _():
+        got_ref[...] = jnp.zeros_like(got_ref)
+
+    @pl.loop(0, columns)
+    def _(c):
+        @pl.loop(1, n_mp)
+        def _(k):
+            col_wait(0, c, k).wait_recv()
+            col_wait(1, c, k).wait_recv()
+
+        standard, inverse = normalize(cols[0, c].reshape(tokens, width).astype(F32))
+        normed = standard.astype(BF16)
+        out_flat = cols[1, c].reshape(tokens, width)
+        lefts[0, c] = normed
+        lefts[1, c] = out_flat
+        query, key, value = (
+            jnp.dot(normed, w_ref[n], preferred_element_type=F32).astype(BF16) for n in range(3))
+        delta = jnp.dot(out_flat, w_ref[3], preferred_element_type=F32).astype(BF16)
+        for t in range(query.shape[1] // LANES):
+            cut = slice(t * LANES, (t + 1) * LANES)
+            results = attend_pair(query[:, cut], key[:, cut], value[:, cut], delta[:, cut])
+            for n in range(4):
+                rights[n, c, :, cut] = results[n]
+
+        @pl.when(sends_back)
+        def _():
+            normed_grad = dot_t(rights[0, c], w_ref[0])
+            normed_grad += dot_t(rights[1, c], w_ref[1])
+            normed_grad += dot_t(rights[2, c], w_ref[2])
+            branch = norm_backward(normed_grad, standard, inverse).astype(BF16)
+            total = (out_flat.astype(F32) + branch.astype(F32)).astype(BF16)
+            back[c] = total.reshape(n_mp, seqs, width)
+
+            @pl.loop(0, n_mp)
+            def _(p):
+                back_copy(c, p).start()
+
+    def weight_grad(slot):
+        left = lefts[slot // 3].reshape(columns * tokens, width)
+        right = rights[slot].reshape(columns * tokens, rights.shape[-1])
+        return t_dot(left, right)
+
+    for j in range(slots):
+        grad = weight_grad((1 - replica) * slots + j)
+        part[j] = grad.reshape(part.shape[1:]).astype(part.dtype)
+        dp_copy(j).start()
+    for j in range(slots):
+        mine[j] = weight_grad(replica * slots + j).reshape(mine.shape[1:])
+    for j in range(slots):
+        dp_copy(j).wait()
+        summed = mine[j] + other[j].astype(F32)
+        mine[j] = summed
+        share[j] = summed.astype(share.dtype)
+
+        @pl.loop(1, n_mp)
+        def _(k):
+            mp_copy(j, k).start()
+
+    for j in range(slots):
+        wout_ref[j] = mine[j, me]
+
+        @pl.loop(1, n_mp)
+        def _(k):
+            mp_wait(j, k).wait_recv()
+            wout_ref[j] += landed[j, source(k)].astype(F32)
+
+    @pl.when(gets_back)
+    def _():
+        @pl.loop(0, columns)
+        def _(c):
+            @pl.loop(0, n_mp)
+            def _(p):
+                back_wait(c, p).wait_recv()
+
+    @pl.when(sends_back)
+    def _():
+        @pl.loop(0, columns)
+        def _(c):
+            @pl.loop(0, n_mp)
+            def _(p):
+                back_copy(c, p).wait_send()
+
+    @pl.loop(1, n_mp)
+    def _(k):
+        @pl.loop(0, columns)
+        def _(c):
+            col_copy(0, c, k).wait_send()
+            col_copy(1, c, k).wait_send()
+
+        for j in range(slots):
+            mp_copy(j, k).wait_send()
+
+
+def per_device_kernel(activations, out_grads, layer_weights):
+    n_mp, n_section, n_dp = (lax.axis_size(name) for name in ("mp", "section", "dp"))
+    _, _, seqs, residues, width = activations.shape
+    columns = residues // n_mp
+    head_width = layer_weights.shape[3]
+    tokens = n_mp * seqs
+    kinds = layer_weights.shape[1]
+    slots, rows = kinds // n_dp, width // n_mp
+
+    def by_column(array):
+        cut = array.reshape(seqs, n_mp, columns, width)
+        return cut.transpose(2, 1, 0, 3)
+
+    vmem = pl.BlockSpec(memory_space=pltpu.VMEM)
+    dma = pltpu.SemaphoreType.DMA
+    pieces = (slots, n_mp, rows, head_width)
+    got, weight_grads = pl.pallas_call(
+        functools.partial(kernel, n_mp, n_section, n_dp),
+        out_shape=(
+            jax.ShapeDtypeStruct((columns, n_mp, seqs, width), BF16),
+            jax.ShapeDtypeStruct((slots, rows, head_width), F32),
+        ),
+        in_specs=[vmem] * 3,
+        out_specs=(vmem, vmem),
+        scratch_shapes=[
+            pltpu.VMEM((2, columns, n_mp, seqs, width), BF16),
+            pltpu.VMEM((2, columns, tokens, width), BF16),
+            pltpu.VMEM((kinds, columns, tokens, head_width), BF16),
+            pltpu.VMEM((columns, n_mp, seqs, width), BF16),
+            pltpu.VMEM(pieces, BF16),
+            pltpu.VMEM(pieces, BF16),
+            pltpu.VMEM(pieces, F32),
+            pltpu.VMEM(pieces, BF16),
+            pltpu.VMEM(pieces, BF16),
+            dma((2, columns, n_mp)),
+            dma((2, columns, n_mp)),
+            dma((columns, n_mp)),
+            dma((columns, n_mp)),
+            dma((slots,)),
+            dma((slots,)),
+            dma((slots, n_mp)),
+            dma((slots, n_mp)),
+        ],
+        compiler_params=pltpu.CompilerParams(
+            collective_id=0, has_side_effects=True, vmem_limit_bytes=48 * 1024 * 1024),
+    )(by_column(activations), by_column(out_grads), layer_weights[0])
+    received = got.transpose(2, 1, 0, 3).reshape(activations.shape)
+    return received, weight_grads[None]
+
+
+def per_device(activations, out_grads, layer_weights):
+    n_mp, n_dp = lax.axis_size("mp"), lax.axis_size("dp")
+    _, kinds, width, head_width = layer_weights.shape
+    fits = (
+        n_dp == 2
+        and kinds % n_dp == 0
+        and n_mp > 1
+        and activations.shape[2] % ROWS == 0
+        and (width // n_mp) % ROWS == 0
+        and head_width % LANES == 0
+    )
+    body = per_device_kernel if fits else per_device_plain
+    return body(activations, out_grads, layer_weights)
+
+
 def solution(mesh):
     in_specs = (
         P("dp", "section", "mp", None, None),

time: 217 us -> 52.6 us (0.24)
  the two profiles are of different devices: /device:TPU:0 before, /device:TPU:10 now
where the time goes in v1:
time: 52.6 us; the launch traced here: 52.4 us
  Pallas kernels  47.7 us (91%)
  local copies, waits for them, and re-layouts  4.02 us (8%)
  between operations  0.67 us (1%)
    pallas_call x1, Pallas kernels, per_device_kernel(): pl.pallas_call(functools.partial(kernel, n_mp, n_section, n_dp), out_shap...  47.7 us
    unnamed x6, local copies, waits for them, and re-layouts  3.9 us

profile of v1, /device:TPU:10, one launch (start us, length us, event | category | flops | bytes accessed | tf_op | source)
XLA Modules:
  0.0 52.4 jit_solution(17429629974188457394)
XLA Ops:
  0.6 1.1 %copy.5 = bf16[1,1,16,32,384]{4,2,3,1,0:T(8,128)(2,1)S(1)} copy(bf16[1,1,16,32,384]{4,3,2,1,0:T(8,128)(2,1)} %param.3) | data formatting | bytes 786432 | tf_op args[0]
  1.8 0.0 copy-start
  1.8 1.2 %copy.7 = bf16[1,1,16,32,384]{4,2,3,1,0:T(8,128)(2,1)S(1)} copy(bf16[1,1,16,32,384]{4,3,2,1,0:T(8,128)(2,1)} %param.4) | data formatting | bytes 786432 | tf_op args[1]
  3.0 0.1 copy_bitcast_fusion
  3.1 0.1 copy-done
  3.1 47.7 %shard_map.50 = (bf16[4,8,16,384]{3,2,1,0:T(8,128)(2,1)S(1)}, f32[2,48,384]{2,1,0:T(8,128)S(1)}) custom-call(bf16[4,8,16,384]{3,2,1,0:T(8,128)(2,1)S(1)} %get-tuple-element.9.acts_ref, bf16[4,8,16,384]{3,2,1,0:T(8,128)(2,1)S(1)} %get-tuple-element.8.grads_ref, bf16[4,384,384]{2,1,0:T(8,128)(2,1)S(1)} %bitcast.10), custom_call_target="tpu_custom_call" | custom-call | tf_op jit(solution)/shard_map/pallas_call | solution.py:396
  50.9 0.8 %copy.10 = bf16[1,1,16,32,384]{4,3,2,1,0:T(8,128)(2,1)} copy(bf16[1,1,16,32,384]{4,2,3,1,0:T(8,128)(2,1)S(1)} %bitcast.13) | data formatting | bytes 786432
  51.8 0.7 %copy.14 = f32[1,2,48,384]{3,2,1,0:T(8,128)} copy(f32[1,2,48,384]{3,2,1,0:T(8,128)S(1)} %bitcast.12) | data formatting | bytes 294912
  (1 shorter events, 0.0 us)
Async XLA Ops:
  1.8 1.4 %copy-start = (bf16[1,4,384,384]{3,2,1,0:T(8,128)(2,1)S(1)}, bf16[1,4,384,384]{3,2,1,0:T(8,128)(2,1)}, u32[]{:S(2)}) copy-start(bf16[1,4,384,384]{3,2,1,0:T(8,128)(2,1)} %param.5) | copy-start | bytes 3538948

commit v2 on v1

--- a/solution.py
+++ b/solution.py
@@ -184,8 +184,8 @@
 
 def kernel(
     n_mp, n_section, n_dp, acts_ref, grads_ref, w_ref, got_ref, wout_ref,
-    cols, lefts, rights, back, part, other, mine, share, landed,
-    col_send, col_recv, back_send, back_recv, dp_send, dp_recv, mp_send, mp_recv,
+    both, cols, lefts, rights, back, part, other, mine, share, landed, total, ysend, yland,
+    col_send, col_recv, back_send, back_recv, dp_send, dp_recv, mp_send, mp_recv, y_send, y_recv,
 ):
     me = lax.axis_index("mp")
     section = lax.axis_index("section")
@@ -196,6 +196,8 @@
     rows = wout_ref.shape[1]
     sends_back = section > 0
     gets_back = section < n_section - 1
+    halves = n_mp // 2
+    half, parity = me // 2, lax.rem(me, 2)
 
     def peer(k):
         return lax.rem(me + k, n_mp)
@@ -203,30 +205,30 @@
     def source(k):
         return lax.rem(me + n_mp - k, n_mp)
 
-    def col_copy(which, c, k):
-        ref = acts_ref if which == 0 else grads_ref
-        return pltpu.make_async_remote_copy(
-            src_ref=ref.at[c, peer(k)], dst_ref=cols.at[which, c, me],
-            send_sem=col_send.at[which, c, k], recv_sem=col_recv.at[which, c, me],
+    others = pl.ds(0, n_mp - 1)
+
+    def col_copy(c, k):
+        return pltpu.make_async_remote_copy(
+            src_ref=both.at[c, peer(k)], dst_ref=cols.at[c, me],
+            send_sem=col_send, recv_sem=col_recv.at[c],
             device_id={"mp": peer(k)}, device_id_type=MESH)
 
-    def col_wait(which, c, k):
-        return pltpu.make_async_remote_copy(
-            src_ref=acts_ref.at[c, me], dst_ref=cols.at[which, c, source(k)],
-            send_sem=col_send.at[which, c, k], recv_sem=col_recv.at[which, c, source(k)],
-            device_id={"mp": peer(k)}, device_id_type=MESH)
+    def col_all(c):
+        return pltpu.make_async_remote_copy(
+            src_ref=both.at[:, others], dst_ref=cols.at[c, others],
+            send_sem=col_send, recv_sem=col_recv.at[c],
+            device_id={"mp": peer(1)}, device_id_type=MESH)
 
     def back_copy(c, p):
         return pltpu.make_async_remote_copy(
             src_ref=back.at[c, p], dst_ref=got_ref.at[c, me],
-            send_sem=back_send.at[c, p], recv_sem=back_recv.at[c, me],
+            send_sem=back_send, recv_sem=back_recv,
             device_id={"section": jnp.maximum(section - 1, 0), "mp": p}, device_id_type=MESH)
 
-    def back_wait(c, p):
-        return pltpu.make_async_remote_copy(
-            src_ref=back.at[c, p], dst_ref=got_ref.at[c, p],
-            send_sem=back_send.at[c, p], recv_sem=back_recv.at[c, p],
-            device_id={"section": jnp.maximum(section - 1, 0), "mp": p}, device_id_type=MESH)
+    def back_all():
+        return pltpu.make_async_remote_copy(
+            src_ref=back, dst_ref=got_ref, send_sem=back_send, recv_sem=back_recv,
+            device_id={"section": jnp.maximum(section - 1, 0)}, device_id_type=MESH)
 
     def dp_copy(j):
         return pltpu.make_async_remote_copy(
@@ -234,17 +236,24 @@
             send_sem=dp_send.at[j], recv_sem=dp_recv.at[j],
             device_id={"dp": 1 - replica}, device_id_type=MESH)
 
+    def y_copy(j):
+        return pltpu.make_async_remote_copy(
+            src_ref=ysend.at[j], dst_ref=yland.at[j],
+            send_sem=y_send.at[j], recv_sem=y_recv.at[j],
+            device_id={"mp": 2 * half + 1 - parity}, device_id_type=MESH)
+
     def mp_copy(j, k):
-        return pltpu.make_async_remote_copy(
-            src_ref=share.at[j, peer(k)], dst_ref=landed.at[j, me],
-            send_sem=mp_send.at[j, k], recv_sem=mp_recv.at[j, me],
-            device_id={"mp": peer(k)}, device_id_type=MESH)
-
-    def mp_wait(j, k):
-        return pltpu.make_async_remote_copy(
-            src_ref=share.at[j, me], dst_ref=landed.at[j, source(k)],
-            send_sem=mp_send.at[j, k], recv_sem=mp_recv.at[j, source(k)],
-            device_id={"mp": peer(k)}, device_id_type=MESH)
+        owner = lax.rem(half + k, halves)
+        return pltpu.make_async_remote_copy(
+            src_ref=share.at[j, owner], dst_ref=landed.at[j, half],
+            send_sem=mp_send, recv_sem=mp_recv.at[j],
+            device_id={"mp": 2 * owner + parity}, device_id_type=MESH)
+
+    def mp_all(j):
+        return pltpu.make_async_remote_copy(
+            src_ref=share.at[:, pl.ds(0, halves - 1)], dst_ref=landed.at[j, pl.ds(0, halves - 1)],
+            send_sem=mp_send, recv_sem=mp_recv.at[j],
+            device_id={"mp": lax.rem(me + 2, n_mp)}, device_id_type=MESH)
 
     barrier = pltpu.get_barrier_semaphore()
 
@@ -268,6 +277,10 @@
             pl.semaphore_signal(
                 barrier, inc=1, device_id={"section": section + 1, "mp": p}, device_id_type=MESH)
 
+    for c in range(columns):
+        both[c, :, 0] = acts_ref[c]
+        both[c, :, 1] = grads_ref[c]
+
     neighbours = (section > 0).astype(jnp.int32) + (section < n_section - 1).astype(jnp.int32)
     pl.semaphore_wait(barrier, n_mp + n_mp * neighbours)
 
@@ -275,13 +288,12 @@
     def _(c):
         @pl.loop(1, n_mp)
         def _(k):
-            col_copy(0, c, k).start()
-            col_copy(1, c, k).start()
-
-    @pl.loop(0, columns)
-    def _(c):
-        cols[0, c, me] = acts_ref[c, me]
-        cols[1, c, me] = grads_ref[c, me]
+            col_copy(c, k).start()
+
+    for c in range(columns):
+        cols[c, me] = both[c, me]
+
+    total[...] = jnp.zeros_like(total)
 
     @pl.when(jnp.logical_not(gets_back))
     def _():
@@ -289,14 +301,10 @@
 
     @pl.loop(0, columns)
     def _(c):
-        @pl.loop(1, n_mp)
-        def _(k):
-            col_wait(0, c, k).wait_recv()
-            col_wait(1, c, k).wait_recv()
-
-        standard, inverse = normalize(cols[0, c].reshape(tokens, width).astype(F32))
+        col_all(c).wait_recv()
+        standard, inverse = normalize(cols[c, :, 0].reshape(tokens, width).astype(F32))
         normed = standard.astype(BF16)
-        out_flat = cols[1, c].reshape(tokens, width)
+        out_flat = cols[c, :, 1].reshape(tokens, width)
         lefts[0, c] = normed
         lefts[1, c] = out_flat
         query, key, value = (
@@ -308,73 +316,72 @@
             for n in range(4):
                 rights[n, c, :, cut] = results[n]
 
+        if columns > 1:
+            @pl.when(c < columns - 1)
+            def _():
+                for n in range(rights.shape[0]):
+                    grad = t_dot(lefts[n // 3, c], rights[n, c])
+                    total[n] += grad
+
         @pl.when(sends_back)
         def _():
             normed_grad = dot_t(rights[0, c], w_ref[0])
             normed_grad += dot_t(rights[1, c], w_ref[1])
             normed_grad += dot_t(rights[2, c], w_ref[2])
             branch = norm_backward(normed_grad, standard, inverse).astype(BF16)
-            total = (out_flat.astype(F32) + branch.astype(F32)).astype(BF16)
-            back[c] = total.reshape(n_mp, seqs, width)
+            grad_in = (out_flat.astype(F32) + branch.astype(F32)).astype(BF16)
+            back[c] = grad_in.reshape(n_mp, seqs, width)
 
             @pl.loop(0, n_mp)
             def _(p):
                 back_copy(c, p).start()
 
-    def weight_grad(slot):
-        left = lefts[slot // 3].reshape(columns * tokens, width)
-        right = rights[slot].reshape(columns * tokens, rights.shape[-1])
-        return t_dot(left, right)
+    def weight_grad(slot, into, j):
+        grad = t_dot(lefts[slot // 3, columns - 1], rights[slot, columns - 1])
+        if columns > 1:
+            grad = grad + total[slot]
+        by_owner = grad.reshape(halves, 2, rows, grad.shape[1]).astype(into.dtype)
+        for y in range(2):
+            into[j, y] = by_owner[:, y]
 
     for j in range(slots):
-        grad = weight_grad((1 - replica) * slots + j)
-        part[j] = grad.reshape(part.shape[1:]).astype(part.dtype)
+        weight_grad((1 - replica) * slots + j, part, j)
         dp_copy(j).start()
     for j in range(slots):
-        mine[j] = weight_grad(replica * slots + j).reshape(mine.shape[1:])
+        weight_grad(replica * slots + j, mine, j)
     for j in range(slots):
         dp_copy(j).wait()
-        summed = mine[j] + other[j].astype(F32)
-        mine[j] = summed
+        ysend[j] = (mine[j, 1 - parity] + other[j, 1 - parity].astype(F32)).astype(BF16)
+        y_copy(j).start()
+        mine[j, parity] += other[j, parity].astype(F32)
+    for j in range(slots):
+        y_copy(j).wait()
+        summed = mine[j, parity] + yland[j].astype(F32)
+        mine[j, parity] = summed
         share[j] = summed.astype(share.dtype)
 
-        @pl.loop(1, n_mp)
+        @pl.loop(1, halves)
         def _(k):
             mp_copy(j, k).start()
 
     for j in range(slots):
-        wout_ref[j] = mine[j, me]
-
-        @pl.loop(1, n_mp)
+        wout_ref[j] = mine[j, parity, half]
+        mp_all(j).wait_recv()
+
+        @pl.loop(1, halves)
         def _(k):
-            mp_wait(j, k).wait_recv()
-            wout_ref[j] += landed[j, source(k)].astype(F32)
+            wout_ref[j] += landed[j, lax.rem(half + halves - k, halves)].astype(F32)
 
     @pl.when(gets_back)
     def _():
-        @pl.loop(0, columns)
-        def _(c):
-            @pl.loop(0, n_mp)
-            def _(p):
-                back_wait(c, p).wait_recv()
+        back_all().wait_recv()
 
     @pl.when(sends_back)
     def _():
-        @pl.loop(0, columns)
-        def _(c):
-            @pl.loop(0, n_mp)
-            def _(p):
-                back_copy(c, p).wait_send()
-
-    @pl.loop(1, n_mp)
-    def _(k):
-        @pl.loop(0, columns)
-        def _(c):
-            col_copy(0, c, k).wait_send()
-            col_copy(1, c, k).wait_send()
-
-        for j in range(slots):
-            mp_copy(j, k).wait_send()
+        back_all().wait_send()
+
+    col_all(0).wait_send()
+    mp_all(0).wait_send()
 
 
 def per_device_kernel(activations, out_grads, layer_weights):
@@ -392,7 +399,8 @@
 
     vmem = pl.BlockSpec(memory_space=pltpu.VMEM)
     dma = pltpu.SemaphoreType.DMA
-    pieces = (slots, n_mp, rows, head_width)
+    pieces = (slots, 2, n_mp // 2, rows, head_width)
+    half_pieces = (slots, n_mp // 2, rows, head_width)
     got, weight_grads = pl.pallas_call(
         functools.partial(kernel, n_mp, n_section, n_dp),
         out_shape=(
@@ -402,23 +410,29 @@
         in_specs=[vmem] * 3,
         out_specs=(vmem, vmem),
         scratch_shapes=[
-            pltpu.VMEM((2, columns, n_mp, seqs, width), BF16),
+            pltpu.VMEM((columns, n_mp, 2, seqs, width), BF16),
+            pltpu.VMEM((columns, n_mp, 2, seqs, width), BF16),
             pltpu.VMEM((2, columns, tokens, width), BF16),
             pltpu.VMEM((kinds, columns, tokens, head_width), BF16),
             pltpu.VMEM((columns, n_mp, seqs, width), BF16),
             pltpu.VMEM(pieces, BF16),
             pltpu.VMEM(pieces, BF16),
             pltpu.VMEM(pieces, F32),
-            pltpu.VMEM(pieces, BF16),
-            pltpu.VMEM(pieces, BF16),
-            dma((2, columns, n_mp)),
-            dma((2, columns, n_mp)),
-            dma((columns, n_mp)),
-            dma((columns, n_mp)),
+            pltpu.VMEM(half_pieces, BF16),
+            pltpu.VMEM(half_pieces, BF16),
+            pltpu.VMEM((kinds, width, head_width), F32),
+            pltpu.VMEM(half_pieces, BF16),
+            pltpu.VMEM(half_pieces, BF16),
+            dma,
+            dma((columns,)),
+            dma,
+            dma,
             dma((slots,)),
             dma((slots,)),
-            dma((slots, n_mp)),
-            dma((slots, n_mp)),
+            dma,
+            dma((slots,)),
+            dma((slots,)),
+            dma((slots,)),
         ],
         compiler_params=pltpu.CompilerParams(
             collective_id=0, has_side_effects=True, vmem_limit_bytes=48 * 1024 * 1024),
@@ -433,7 +447,7 @@
     fits = (
         n_dp == 2
         and kinds % n_dp == 0
-        and n_mp > 1
+        and n_mp % 2 == 0
         and activations.shape[2] % ROWS == 0
         and (width // n_mp) % ROWS == 0
         and head_width % LANES == 0

time: 52.6 us -> 50 us (0.951)
  the two profiles are of different devices: /device:TPU:10 before, /device:TPU:0 now
where the time goes in v2:
time: 50 us; the launch traced here: 49.9 us
  Pallas kernels  45.2 us (90%)
  local copies, waits for them, and re-layouts  4.02 us (8%)
  between operations  0.67 us (1%)
    pallas_call x1, Pallas kernels, per_device_kernel(): pl.pallas_call(functools.partial(kernel, n_mp, n_section, n_dp), out_shap...  45.2 us
    unnamed x6, local copies, waits for them, and re-layouts  3.9 us

profile of v2, /device:TPU:0, one launch (start us, length us, event | category | flops | bytes accessed | tf_op | source)
XLA Modules:
  0.0 49.9 jit_solution(15390563449471347336)
XLA Ops:
  0.6 1.1 %copy.5 = bf16[1,1,16,32,384]{4,2,3,1,0:T(8,128)(2,1)S(1)} copy(bf16[1,1,16,32,384]{4,3,2,1,0:T(8,128)(2,1)} %param.3) | data formatting | bytes 786432 | tf_op args[0]
  1.8 0.0 copy-start
  1.8 1.2 %copy.7 = bf16[1,1,16,32,384]{4,2,3,1,0:T(8,128)(2,1)S(1)} copy(bf16[1,1,16,32,384]{4,3,2,1,0:T(8,128)(2,1)} %param.4) | data formatting | bytes 786432 | tf_op args[1]
  3.0 0.1 copy_bitcast_fusion
  3.1 0.1 copy-done
  3.1 45.2 %shard_map.50 = (bf16[4,8,16,384]{3,2,1,0:T(8,128)(2,1)S(1)}, f32[2,48,384]{2,1,0:T(8,128)S(1)}) custom-call(bf16[4,8,16,384]{3,2,1,0:T(8,128)(2,1)S(1)} %get-tuple-element.9.acts_ref, bf16[4,8,16,384]{3,2,1,0:T(8,128)(2,1)S(1)} %get-tuple-element.8.grads_ref, bf16[4,384,384]{2,1,0:T(8,128)(2,1)S(1)} %bitcast.10), custom_call_target="tpu_custom_call" | custom-call | tf_op jit(solution)/shard_map/pallas_call | solution.py:404
  48.4 0.8 %copy.10 = bf16[1,1,16,32,384]{4,3,2,1,0:T(8,128)(2,1)} copy(bf16[1,1,16,32,384]{4,2,3,1,0:T(8,128)(2,1)S(1)} %bitcast.13) | data formatting | bytes 786432
  49.2 0.7 %copy.14 = f32[1,2,48,384]{3,2,1,0:T(8,128)} copy(f32[1,2,48,384]{3,2,1,0:T(8,128)S(1)} %bitcast.12) | data formatting | bytes 294912
  (1 shorter events, 0.0 us)
Async XLA Ops:
  1.8 1.4 %copy-start = (bf16[1,4,384,384]{3,2,1,0:T(8,128)(2,1)S(1)}, bf16[1,4,384,384]{3,2,1,0:T(8,128)(2,1)}, u32[]{:S(2)}) copy-start(bf16[1,4,384,384]{3,2,1,0:T(8,128)(2,1)} %param.5) | copy-start | bytes 3538948

commit v3 on v2

--- a/solution.py
+++ b/solution.py
@@ -194,6 +194,7 @@
     tokens = n_mp * seqs
     slots = wout_ref.shape[0]
     rows = wout_ref.shape[1]
+    lane_tiles = wout_ref.shape[2] // LANES
     sends_back = section > 0
     gets_back = section < n_section - 1
     halves = n_mp // 2
@@ -236,16 +237,19 @@
             send_sem=dp_send.at[j], recv_sem=dp_recv.at[j],
             device_id={"dp": 1 - replica}, device_id_type=MESH)
 
-    def y_copy(j):
-        return pltpu.make_async_remote_copy(
-            src_ref=ysend.at[j], dst_ref=yland.at[j],
-            send_sem=y_send.at[j], recv_sem=y_recv.at[j],
+    def lanes(t):
+        return pl.ds(t * LANES, LANES)
+
+    def y_copy(j, t):
+        return pltpu.make_async_remote_copy(
+            src_ref=ysend.at[j, :, :, lanes(t)], dst_ref=yland.at[j, :, :, lanes(t)],
+            send_sem=y_send.at[j, t], recv_sem=y_recv.at[j, t],
             device_id={"mp": 2 * half + 1 - parity}, device_id_type=MESH)
 
-    def mp_copy(j, k):
+    def mp_copy(j, t, k):
         owner = lax.rem(half + k, halves)
         return pltpu.make_async_remote_copy(
-            src_ref=share.at[j, owner], dst_ref=landed.at[j, half],
+            src_ref=share.at[j, owner, :, lanes(t)], dst_ref=landed.at[j, half, :, lanes(t)],
             send_sem=mp_send, recv_sem=mp_recv.at[j],
             device_id={"mp": 2 * owner + parity}, device_id_type=MESH)
 
@@ -352,17 +356,17 @@
     for j in range(slots):
         dp_copy(j).wait()
         ysend[j] = (mine[j, 1 - parity] + other[j, 1 - parity].astype(F32)).astype(BF16)
-        y_copy(j).start()
+        for t in range(lane_tiles):
+            y_copy(j, t).start()
         mine[j, parity] += other[j, parity].astype(F32)
     for j in range(slots):
-        y_copy(j).wait()
-        summed = mine[j, parity] + yland[j].astype(F32)
-        mine[j, parity] = summed
-        share[j] = summed.astype(share.dtype)
-
-        @pl.loop(1, halves)
-        def _(k):
-            mp_copy(j, k).start()
+        for t in range(lane_tiles):
+            y_copy(j, t).wait()
+            summed = mine[j, parity, :, :, lanes(t)] + yland[j, :, :, lanes(t)].astype(F32)
+            mine[j, parity, :, :, lanes(t)] = summed
+            share[j, :, :, lanes(t)] = summed.astype(share.dtype)
+            for k in range(1, halves):
+                mp_copy(j, t, k).start()
 
     for j in range(slots):
         wout_ref[j] = mine[j, parity, half]
@@ -431,8 +435,8 @@
             dma((slots,)),
             dma,
             dma((slots,)),
-            dma((slots,)),
-            dma((slots,)),
+            dma((slots, head_width // LANES)),
+            dma((slots, head_width // LANES)),
         ],
         compiler_params=pltpu.CompilerParams(
             collective_id=0, has_side_effects=True, vmem_limit_bytes=48 * 1024 * 1024),

time: 50 us -> 49.5 us (0.990)
  Pallas kernels: 45.2 us -> 44.6 us
    pallas_call x1, Pallas kernels: 45.2 us -> 44.6 us  [per_device_kernel(): pl.pallas_call(functools.partial(kernel, n_mp, n_section, n_dp), out_shap...]
where the time goes in v3:
time: 49.5 us; the launch traced here: 49.3 us
  Pallas kernels  44.6 us (90%)
  local copies, waits for them, and re-layouts  4.02 us (8%)
  between operations  0.67 us (1%)
    pallas_call x1, Pallas kernels, per_device_kernel(): pl.pallas_call(functools.partial(kernel, n_mp, n_section, n_dp), out_shap...  44.6 us
    unnamed x6, local copies, waits for them, and re-layouts  3.9 us

profile of v3, /device:TPU:0, one launch (start us, length us, event | category | flops | bytes accessed | tf_op | source)
XLA Modules:
  0.0 49.3 jit_solution(9177659199969492486)
XLA Ops:
  0.6 1.1 %copy.5 = bf16[1,1,16,32,384]{4,2,3,1,0:T(8,128)(2,1)S(1)} copy(bf16[1,1,16,32,384]{4,3,2,1,0:T(8,128)(2,1)} %param.3) | data formatting | bytes 786432 | tf_op args[0]
  1.8 0.0 copy-start
  1.8 1.2 %copy.7 = bf16[1,1,16,32,384]{4,2,3,1,0:T(8,128)(2,1)S(1)} copy(bf16[1,1,16,32,384]{4,3,2,1,0:T(8,128)(2,1)} %param.4) | data formatting | bytes 786432 | tf_op args[1]
  3.0 0.1 copy_bitcast_fusion
  3.1 0.1 copy-done
  3.1 44.6 %shard_map.50 = (bf16[4,8,16,384]{3,2,1,0:T(8,128)(2,1)S(1)}, f32[2,48,384]{2,1,0:T(8,128)S(1)}) custom-call(bf16[4,8,16,384]{3,2,1,0:T(8,128)(2,1)S(1)} %get-tuple-element.9.acts_ref, bf16[4,8,16,384]{3,2,1,0:T(8,128)(2,1)S(1)} %get-tuple-element.8.grads_ref, bf16[4,384,384]{2,1,0:T(8,128)(2,1)S(1)} %bitcast.10), custom_call_target="tpu_custom_call" | custom-call | tf_op jit(solution)/shard_map/pallas_call | solution.py:408
  47.8 0.8 %copy.10 = bf16[1,1,16,32,384]{4,3,2,1,0:T(8,128)(2,1)} copy(bf16[1,1,16,32,384]{4,2,3,1,0:T(8,128)(2,1)S(1)} %bitcast.13) | data formatting | bytes 786432
  48.6 0.7 %copy.14 = f32[1,2,48,384]{3,2,1,0:T(8,128)} copy(f32[1,2,48,384]{3,2,1,0:T(8,128)S(1)} %bitcast.12) | data formatting | bytes 294912
  (1 shorter events, 0.0 us)
Async XLA Ops:
  1.8 1.4 %copy-start = (bf16[1,4,384,384]{3,2,1,0:T(8,128)(2,1)S(1)}, bf16[1,4,384,384]{3,2,1,0:T(8,128)(2,1)}, u32[]{:S(2)}) copy-start(bf16[1,4,384,384]{3,2,1,0:T(8,128)(2,1)} %param.5) | copy-start | bytes 3538948
